TPU v7x, 32 devices: a whole 2x2x4 slice. The times are simulated.
32 devices in a mesh: grp: 4 (over y, core), mem: 8 (over z, x).
Axes of the slice: x: 2, y: 2, z: 4, core: 2. Of those that a mesh axis runs over, the one named last changes fastest.
Arguments:
- vectors: bfloat16 [32768, 768], P(('grp', 'mem')), may hold values from -6 to 6
- parents: int32 [32768], P(('grp', 'mem')), may hold values from 0 to 1
- children: int32 [32768], P(('grp', 'mem')), may hold values from 0 to 1023
- counts: int32 [32, 4], P(('grp', 'mem')), may hold values from 85 to 512, as said below
Outputs:
- distances: float32 [65536, 1024], P(('grp', 'mem'))
Inputs may be any that keep to these rules, and one draw needn't show every extreme that they name: Each row of counts sums to 1024; shard d's vectors go to group 0 first, then group 1, and so on, in that many rows each. In every draw some group receives 512 vectors from every storage shard.
All inputs are finite; a program needn't handle non-finite values.
Results may differ from a plain program's by a relative error of at most 0.00055.
Values may be sent and summed in bfloat16 or wider, within the bound.
A program may use at most 128 MiB of HBM per device.

v0:
```python
import math

import jax
import jax.numpy as jnp
from jax import lax
from jax.sharding import PartitionSpec as P

D = 768
CHILD = 1024
PAR_GRP = 2


def pick_parent(all_dists, row_codes):
    row_count = all_dists.shape[0]
    stacked = all_dists.reshape(row_count, PAR_GRP, CHILD)
    parent_ids = jnp.maximum(row_codes, 0) // CHILD
    chosen = parent_ids[:, None, None] == jnp.arange(PAR_GRP, dtype=jnp.int32)[None, :, None]
    picked = jnp.sum(jnp.where(chosen, stacked, jnp.zeros((), jnp.float32)), axis=1)
    return jnp.where(row_codes[:, None] >= 0, picked, jnp.zeros((), jnp.float32))


def column_block(centroids, vec_norm, arrived):
    cent_wide = centroids.astype(jnp.float32)
    cent_norm = jnp.sum(cent_wide * cent_wide, axis=1)
    cross = lax.dot_general(
        arrived, centroids, (((1,), (1,)), ((), ())), preferred_element_type=jnp.float32
    )
    return (vec_norm[:, None] - 2.0 * cross + cent_norm[None, :]) / D


def body(vectors, parents, children, counts):
    groups = lax.axis_size("grp")
    vec_rows = vectors.shape[0]
    capacity = 2 * vec_rows // groups
    width = PAR_GRP * CHILD
    send_counts = counts[0]
    offsets = jnp.cumsum(send_counts) - send_counts
    slots = jnp.arange(capacity, dtype=jnp.int32)
    filled = slots[None, :] < send_counts[:, None]
    source_rows = jnp.where(filled, offsets[:, None] + slots[None, :], 0).reshape(-1)
    flat_filled = filled.reshape(-1)
    outgoing_rows = jnp.where(
        flat_filled[:, None], jnp.take(vectors, source_rows, axis=0), jnp.zeros((), jnp.bfloat16)
    )
    outgoing_rows = outgoing_rows.reshape(groups, capacity, D)
    row_codes = jnp.take(parents, source_rows) * CHILD + jnp.take(children, source_rows)
    row_codes = jnp.where(flat_filled, row_codes, -1).reshape(groups, capacity)
    arrived, arrived_codes = (
        lax.all_to_all(outgoing_rows, "grp", split_axis=0, concat_axis=0, tiled=True),
        lax.all_to_all(row_codes, "grp", split_axis=0, concat_axis=0, tiled=True),
    )
    row_total = groups * capacity
    arrived = arrived.reshape(row_total, D)
    arrived_codes = arrived_codes.reshape(row_total)
    block_rows = math.gcd(row_total, 512)
    column_ids = jnp.arange(width, dtype=jnp.int32)

    def add_into_totals(running, block_pair):
        block_vecs, block_codes = block_pair
        onehot = (block_codes[:, None] == column_ids[None, :]).astype(jnp.bfloat16)
        new_sums = running[0] + lax.dot_general(
            onehot, block_vecs, (((0,), (0,)), ((), ())), preferred_element_type=jnp.float32
        )
        tallies = running[1] + jnp.sum(onehot, axis=0, dtype=jnp.float32)
        return ((new_sums, tallies), None)

    start_state = (jnp.zeros((width, D), jnp.float32), jnp.zeros((width,), jnp.float32))
    blocked = (
        arrived.reshape(row_total // block_rows, block_rows, D),
        arrived_codes.reshape(row_total // block_rows, block_rows),
    )
    (child_sums, child_counts), unused = lax.scan(add_into_totals, start_state, blocked)
    vec_wide = arrived.astype(jnp.float32)
    vec_norm = jnp.sum(vec_wide * vec_wide, axis=1)
    totals, tallies = (
        lax.psum(child_sums.astype(jnp.bfloat16), "mem").astype(jnp.float32),
        lax.psum(child_counts.astype(jnp.bfloat16), "mem").astype(jnp.float32),
    )
    centroids = (totals / jnp.maximum(tallies, 1.0)[:, None]).astype(jnp.bfloat16)
    all_dists = column_block(centroids, vec_norm, arrived)
    return pick_parent(all_dists, arrived_codes)


def solution(mesh):
    in_specs = (
        P(("grp", "mem"), None),
        P(("grp", "mem")),
        P(("grp", "mem")),
        P(("grp", "mem"), None),
    )
    out_specs = P(("grp", "mem"), None)
    return jax.shard_map(body, mesh=mesh, in_specs=in_specs, out_specs=out_specs, check_vma=False)
```

profile of v0, /device:TPU:12, one launch (start us, length us, event | category | flops | bytes accessed | tf_op | source)
XLA Modules:
  0.0 294.4 jit_solution(8874099648105566454)
XLA Ops:
  6.5 1.0 reduce-window.8
  8.2 0.7 iota_compare_fusion.5
  8.9 0.7 fusion.11
  9.7 10.2 %gather_fusion.2 = s32[2048]{0:T(1024)S(1)} fusion(s32[1024]{0:T(1024)} %param.10, s32[2048]{0:T(1024)S(1)} %fusion.12), kind=kCustom, calls=%fused_computation.1.clone | custom fusion | bytes 24576 | tf_op jit(solution)/shard_map/jit(_take)/gather | solution.py:46
  19.9 8.6 %gather_fusion.1 = s32[2048]{0:T(1024)S(1)} fusion(s32[1024]{0:T(1024)S(1)} %copy-done.1, s32[2048]{0:T(1024)S(1)} %fusion.12), kind=kCustom, calls=%fused_computation.clone | custom fusion | bytes 24576 | tf_op jit(solution)/shard_map/jit(_take)/gather | solution.py:46
  29.1 3.7 %all-to-all-start = ((s32[4,1,512]{2,1,0:T(1,128)}), s32[4,1,512]{2,1,0:T(1,128)S(1)}, u32[]{:S(2)}, u32[]{:S(2)}) async-start(s32[4,1,512]{2,1,0:T(1,128)} %bitcast.3), calls=%async_computation | async-start | bytes 16384 | tf_op jit(solution)/shard_map/all_to_all | solution.py:50
  32.9 9.4 %gather_fusion = bf16[2048,768]{1,0:T(8,128)(2,1)} fusion(bf16[1024,768]{1,0:T(8,128)(2,1)S(1)} %copy-done, s32[2048]{0:T(1024)S(1)} %broadcast_clamp_fusion), kind=kCustom, calls=%fused_computation.2 | custom fusion | bytes 6299648 | tf_op jit(solution)/shard_map/jit(_take)/gather | solution.py:43
  42.3 3.4 %select_select_fusion = bf16[4,512,768]{2,1,0:T(8,128)(2,1)} fusion(bf16[4,512,768]{2,1,0:T(8,128)(2,1)} %bitcast.41, pred[4,512]{1,0:T(4,128)(4,1)S(1)} %get-tuple-element.75, pred[4,512]{1,0:T(4,128)(4,1)S(1)} %get-tuple-element.73), kind=kLoop, calls=%fused_computation.21 | loop fusion | flops 3145728 | bytes 6295552 | tf_op jit(solution)/shard_map/jit(_where)/select_n | solution.py:42
  45.7 4.6 %all-to-all-start.1 = ((bf16[4,512,768]{2,1,0:T(8,128)(2,1)}), bf16[4,512,768]{2,1,0:T(8,128)(2,1)}, u32[]{:S(2)}, u32[]{:S(2)}) async-start(bf16[4,512,768]{2,1,0:T(8,128)(2,1)} %select_select_fusion), calls=%async_computation.1 | async-start | bytes 6291456 | tf_op jit(solution)/shard_map/all_to_all | solution.py:49
  50.4 35.3 %all-to-all-done.1 = bf16[4,512,768]{2,1,0:T(8,128)(2,1)} async-done(((bf16[4,512,768]{2,1,0:T(8,128)(2,1)}), bf16[4,512,768]{2,1,0:T(8,128)(2,1)}, u32[]{:S(2)}, u32[]{:S(2)}) %all-to-all-start.1) | async-done | bytes 3145760 | tf_op jit(solution)/shard_map/all_to_all | solution.py:49
  85.7 31.2 %while.13 = (s32[]{:T(128)}, f32[2048,768]{1,0:T(8,128)}, f32[2048]{0:T(1024)S(1)}, s32[4,512]{1,0:T(4,128)S(1)}, bf16[4,512,768]{2,1,0:T(8,128)(2,1)}, /*index=5*/s32[]{:T(128)}, s32[]{:T(128)}) while((s32[]{:T(128)}, f32[2048,768]{1,0:T(8,128)}, f32[2048]{0:T(1024)S(1)}, s32[4,512]{1,0:T(4,128)S(1)}, ...), condition=%wide.region_4.6_spmd.clone, body=%wide.region_2.5_spmd.clone.sunk | while | flops 1619003392 | bytes 13410408 | solution.py:72
  86.3 5.8 %select_add_fusion.5 = f32[2048,768]{1,0:T(8,128)} fusion(f32[2048,768]{1,0:T(8,128)} %get-tuple-element.117, pred[]{:T(512)S(6)} %compare.7, s32[512]{0:T(512)S(1)} %bitcast.43, bf16[4,512,768]{2,1,0:T(8,128)(2,1)} %get-tuple-element.127, s32[]{:T(128)S(6)} %copy.20), kind=kOutput, calls=%fused_computation.4.clone.1 | convolution fusion | flops 1614807040 | bytes 13371397 | tf_op jit(solution)/shard_map/while/body/eval_jaxpr/dot_general | solution.py:61
  92.7 7.7 %select_add_fusion.5 = f32[2048,768]{1,0:T(8,128)} fusion(f32[2048,768]{1,0:T(8,128)} %get-tuple-element.117, pred[]{:T(512)S(6)} %compare.7, s32[512]{0:T(512)S(1)} %bitcast.43, bf16[4,512,768]{2,1,0:T(8,128)(2,1)} %get-tuple-element.127, s32[]{:T(128)S(6)} %copy.20), kind=kOutput, calls=%fused_computation.4.clone.1 | convolution fusion | flops 1614807040 | bytes 13371397 | tf_op jit(solution)/shard_map/while/body/eval_jaxpr/dot_general | solution.py:61
  101.0 7.7 %select_add_fusion.5 = f32[2048,768]{1,0:T(8,128)} fusion(f32[2048,768]{1,0:T(8,128)} %get-tuple-element.117, pred[]{:T(512)S(6)} %compare.7, s32[512]{0:T(512)S(1)} %bitcast.43, bf16[4,512,768]{2,1,0:T(8,128)(2,1)} %get-tuple-element.127, s32[]{:T(128)S(6)} %copy.20), kind=kOutput, calls=%fused_computation.4.clone.1 | convolution fusion | flops 1614807040 | bytes 13371397 | tf_op jit(solution)/shard_map/while/body/eval_jaxpr/dot_general | solution.py:61
  109.3 7.7 %select_add_fusion.5 = f32[2048,768]{1,0:T(8,128)} fusion(f32[2048,768]{1,0:T(8,128)} %get-tuple-element.117, pred[]{:T(512)S(6)} %compare.7, s32[512]{0:T(512)S(1)} %bitcast.43, bf16[4,512,768]{2,1,0:T(8,128)(2,1)} %get-tuple-element.127, s32[]{:T(128)S(6)} %copy.20), kind=kOutput, calls=%fused_computation.4.clone.1 | convolution fusion | flops 1614807040 | bytes 13371397 | tf_op jit(solution)/shard_map/while/body/eval_jaxpr/dot_general | solution.py:61
  116.9 4.8 %convert_element_type.29 = bf16[2048,768]{1,0:T(8,128)(2,1)} convert(f32[2048,768]{1,0:T(8,128)} %get-tuple-element.39) | non-fusion elementwise | flops 1572864 | bytes 9437184 | tf_op jit(solution)/shard_map/convert_element_type | solution.py:76
  121.9 2.6 multiply_reduce_fusion.1
  124.5 19.6 %psum.15 = bf16[2048]{0:T(1024)(128)(2,1)S(1)} all-reduce(bf16[2048]{0:T(1024)(128)(2,1)S(1)} %convert_element_type.31), channel_id=1, replica_groups=mesh['grp'=4,'mem'=8] {'mem'}, use_global_device_ids=true, to_apply=%region_6.8 | all-reduce | flops 2048 | bytes 8192 | tf_op jit(solution)/shard_map/psum | solution.py:77
  144.1 106.7 %all-reduce.2.cloned.1.call-done = bf16[2048,768]{1,0:T(8,128)(2,1)} async-done(((bf16[2048,768]{1,0:T(8,128)(2,1)}), bf16[2048,768]{1,0:T(8,128)(2,1)}) %all-reduce.2.cloned.1.call-update) | async-done | bytes 3145744 | tf_op jit(solution)/shard_map/psum | solution.py:76
  250.9 2.6 multiply_reduce_fusion
  253.4 12.7 %add_multiply_fusion = f32[2048,2048]{0,1:T(8,128)} fusion(f32[2048]{0:T(1024)S(1)} %multiply_reduce_fusion, f32[2048]{0:T(1024)S(1)} %bitcast.55, bf16[2048,768]{1,0:T(8,128)(2,1)} %bitcast.7, bf16[2048,768]{1,0:T(8,128)(2,1)} %all-reduce.2.cloned.1.call-done, f32[2048]{0:T(1024)S(1)} %convert_maximum_fusion), kind=kOutput, calls=%fused_computation.16 | convolution fusion | flops 6463946752 | bytes 23093248 | tf_op jit(solution)/shard_map/dot_general | solution.py:25
  266.1 8.0 %select_reduce_fusion = f32[2048,1024]{0,1:T(8,128)S(1)} fusion(f32[2048,2,1024]{0,2,1:T(8,128)} %bitcast.40, pred[2048,2]{0,1:T(4,128)(4,1)S(1)} %iota_compare_fusion.4), kind=kLoop, calls=%fused_computation.15 | loop fusion | flops 6291456 | bytes 25169920 | tf_op jit(solution)/shard_map/reduce_sum | solution.py:18
  274.2 4.1 %broadcast_select_fusion = f32[2048,1024]{0,1:T(8,128)} fusion(f32[2048,1024]{0,1:T(8,128)S(1)} %select_reduce_fusion, pred[2048]{0:T(1024)(128)(4,1)S(1)} %bitcast.53), kind=kLoop, calls=%fused_computation.20 | loop fusion | flops 2097152 | bytes 16779264 | tf_op jit(solution)/shard_map/jit(_where)/select_n | solution.py:19
  278.3 9.2 %copy.7 = f32[2048,1024]{1,0:T(8,128)} copy(f32[2048,1024]{0,1:T(8,128)} %broadcast_select_fusion) | data formatting | bytes 16777216 | tf_op jit(solution)/shard_map/jit(_where)/select_n | solution.py:19
  (39 shorter events, 3.8 us)
Async XLA Ops:
  6.5 26.3 %copy-start = (bf16[1024,768]{1,0:T(8,128)(2,1)S(1)}, bf16[1024,768]{1,0:T(8,128)(2,1)}, u32[]{:S(2)}) copy-start(bf16[1024,768]{1,0:T(8,128)(2,1)} %param.8) | copy-start | bytes 4718596
  6.5 13.4 %copy-start.1 = (s32[1024]{0:T(1024)S(1)}, s32[1024]{0:T(1024)}, u32[]{:S(2)}) copy-start(s32[1024]{0:T(1024)} %param.9) | copy-start | bytes 12292
  29.1 16.6 %all-to-all-start = ((s32[4,1,512]{2,1,0:T(1,128)}), s32[4,1,512]{2,1,0:T(1,128)S(1)}, u32[]{:S(2)}, u32[]{:S(2)}) async-start(s32[4,1,512]{2,1,0:T(1,128)} %bitcast.3), calls=%async_computation | async-start | bytes 16384 | tf_op jit(solution)/shard_map/all_to_all | solution.py:50
  45.7 40.0 %all-to-all-start.1 = ((bf16[4,512,768]{2,1,0:T(8,128)(2,1)}), bf16[4,512,768]{2,1,0:T(8,128)(2,1)}, u32[]{:S(2)}, u32[]{:S(2)}) async-start(bf16[4,512,768]{2,1,0:T(8,128)(2,1)} %select_select_fusion), calls=%async_computation.1 | async-start | bytes 6291456 | tf_op jit(solution)/shard_map/all_to_all | solution.py:49
  50.3 200.5 %all-reduce.2.cloned.1.call-start = ((), (), s32[]{:S(2)}) async-start(), calls=%async_computation.2 | async-start | bytes 6291456 | tf_op jit(solution)/shard_map/psum | solution.py:76
Sparse Core Ops, SparseCore 0:
  121.8 128.9 all-reduce.1
where the time goes:
time: 298 us; the launch traced here: 294 us
  waiting for transfers between devices  142 us (48%)
  matrix products  41.5 us (14%)
  local copies, waits for them, and re-layouts  37.5 us (13%)
  other arithmetic  31.6 us (11%)
  blocking collectives  19.6 us (7%)
  between operations  13.6 us (5%)
  starting transfers between devices  8.38 us (3%)
    psum x1, waiting for transfers between devices, body(): lax.psum(child_sums.astype(jnp.bfloat16), 'mem').astype(jnp.float32)  107 us
    all_to_all x1, waiting for transfers between devices, body(): lax.all_to_all(outgoing_rows, 'grp', split_axis=0, concat_axis=0, tiled=T...  35.3 us
    dot_general x4, matrix products, add_into_totals(): lax.dot_general(onehot, block_vecs, (((0,), (0,)), ((), ())), preferred_e...  28.8 us
    psum x1, blocking collectives, body(): lax.psum(child_counts.astype(jnp.bfloat16), 'mem').astype(jnp.float32)  19.6 us
    dot_general x1, matrix products, column_block(): lax.dot_general(arrived, centroids, (((1,), (1,)), ((), ())), preferred_e...  12.7 us
    gather x1, local copies, waits for them, and re-layouts, body(): jnp.take(children, source_rows)  10.2 us
    gather x1, local copies, waits for them, and re-layouts, body(): jnp.take(vectors, source_rows, axis=0)  9.4 us
    select_n x1, local copies, waits for them, and re-layouts, pick_parent(): jnp.where(row_codes[:, None] >= 0, picked, jnp.zeros((), jnp.float32))  9.24 us
  transfers between devices with their start and end apart: 3, of which 2 were waited for; matrix products, arithmetic and copies ran while one was open for 5% of the time, Pallas kernels for 0%

commit v1 on v0

v1 whole, which is shorter than its diff:
```python
import functools

import jax
import jax.numpy as jnp
from jax import lax
from jax.experimental import pallas as pl
from jax.experimental.pallas import tpu as pltpu
from jax.sharding import PartitionSpec as P

CHILD = 1024
PAR_GRP = 2
WIDTH = PAR_GRP * CHILD
LOW = 32
MIB = 1024 * 1024


def inner_size(members):
    return max(d for d in range(1, members + 1) if members % d == 0 and d * d <= members)


def exchange_kernel(
    dims,
    counts_ref,
    vec_ref,
    par_ref,
    chi_ref,
    arr_out,
    cent_out,
    code_out,
    pick,
    out_codes,
    in_codes,
    group_codes,
    outgoing,
    arrived,
    member,
    sums,
    x_in,
    half,
    z_in,
    cent,
    sem_code,
    sem_vec,
    sem_xcode,
    sem_zcode,
    sem_x,
    sem_z,
    sem_zc,
    sem_xc,
    sem_local,
):
    groups, inner, outer, rows, cap, blocks, cols = dims
    slots = groups * cap
    share = WIDTH // inner
    part = share // outer
    g = lax.axis_index("grp")
    m = lax.axis_index("mem")
    zi, xi = m // inner, m % inner

    def grp_at(t):
        return (g + t) % groups

    def x_dev(t):
        return {"mem": zi * inner + (xi + t) % inner}

    def z_dev(t):
        return {"mem": ((zi + t) % outer) * inner + xi}

    barrier = pltpu.get_barrier_semaphore()
    for t in range(1, groups):
        pl.semaphore_signal(barrier, inc=1, device_id={"grp": grp_at(t)}, device_id_type=pl.DeviceIdType.MESH)
    for t in range(1, inner):
        pl.semaphore_signal(barrier, inc=1, device_id=x_dev(t), device_id_type=pl.DeviceIdType.MESH)
    for t in range(1, outer):
        pl.semaphore_signal(barrier, inc=1, device_id=z_dev(t), device_id_type=pl.DeviceIdType.MESH)

    def remote(src, dst, sems, where, device):
        return pltpu.make_async_remote_copy(
            src_ref=src,
            dst_ref=dst,
            send_sem=sems.at[(0,) + where],
            recv_sem=sems.at[(1,) + where],
            device_id=device,
            device_id_type=pl.DeviceIdType.MESH,
        )

    sent = []
    kept = []

    def send(*what):
        copy = remote(*what)
        copy.start()
        sent.append(copy)

    def keep(src, dst, number):
        copy = pltpu.make_async_copy(src, dst, sem_local.at[number])
        copy.start()
        kept.append(copy)

    code = par_ref[...] * CHILD + chi_ref[...]
    high = (code // LOW + 1).astype(jnp.float32)
    low = (code % LOW).astype(jnp.float32)
    first = lax.broadcasted_iota(jnp.int32, (16, rows), 0) == 0
    code_rows = jnp.where(first, high, low).astype(jnp.bfloat16)
    step = min(cap, 256)

    def make_pick(t):
        h = grp_at(t)
        count = counts_ref[0, h]
        offset = jnp.int32(0)
        for other in range(groups):
            offset = offset + jnp.where(other < h, counts_ref[0, other], 0)
        for base in range(0, cap, step):
            slot = lax.broadcasted_iota(jnp.int32, (step, rows), 0) + base
            row = lax.broadcasted_iota(jnp.int32, (step, rows), 1)
            chosen = jnp.logical_and(row - slot == offset, slot < count)
            pick[t, base : base + step, :] = jnp.where(chosen, 1.0, 0.0).astype(jnp.bfloat16)
        got = lax.dot_general(
            code_rows, pick[t], (((1,), (1,)), ((), ())), preferred_element_type=jnp.float32
        )
        value = (got[0:1] * LOW + got[1:2] - LOW).astype(jnp.int32)
        return jnp.broadcast_to(value, (8, cap))

    def picked(t, q):
        return jnp.dot(
            pick[t], vec_ref[:, q * cols : (q + 1) * cols], preferred_element_type=jnp.float32
        ).astype(jnp.bfloat16)

    def send_rows(t, q):
        outgoing[q, t - 1] = picked(t, q)
        send(outgoing.at[q, t - 1], arrived.at[q, g], sem_vec, (q, t - 1), {"grp": grp_at(t)})

    order = sorted(range(1, groups), key=lambda t: abs(2 * t - groups))
    for place, t in enumerate(order):
        out_codes[t - 1] = make_pick(t)
        outgoing[0, t - 1] = picked(t, 0)
        if place == 0:
            pl.semaphore_wait(barrier, groups + inner + outer - 3)
        send(out_codes.at[t - 1], in_codes.at[g], sem_code, (t - 1,), {"grp": grp_at(t)})
        send(outgoing.at[0, t - 1], arrived.at[0, g], sem_vec, (0, t - 1), {"grp": grp_at(t)})
    in_codes[g] = make_pick(0)
    arrived[0, g] = picked(0, 0)
    for q in range(1, blocks):
        for t in order:
            send_rows(t, q)
        arrived[q, g] = picked(0, q)

    for t in order:
        s = (g - t + groups) % groups
        remote(in_codes.at[s], in_codes.at[s], sem_code, (t - 1,), {"grp": grp_at(t)}).wait_recv()
    lanes = lax.broadcasted_iota(jnp.int32, group_codes.shape[2:], 0)
    mine = jnp.full(group_codes.shape[2:], -1, jnp.int32)
    for s in range(groups):
        mine = jnp.where(lanes == s, jnp.broadcast_to(in_codes[s, 0:1, :], mine.shape), mine)
    group_codes[0, 0] = mine
    for t in range(1, inner):
        send(group_codes.at[0, 0], group_codes.at[0, t], sem_xcode, (t - 1,), x_dev(t))
    keep(group_codes.at[0, 0], code_out, 0)

    tall = 256

    @pl.loop(0, WIDTH // tall)
    def _(i):
        ids = lax.broadcasted_iota(jnp.int32, (tall, cap), 0) + i * tall
        for s in range(groups):
            hit = ids == in_codes[s, 0:1, :]
            member[pl.ds(pl.multiple_of(i * tall, tall), tall), s * cap : (s + 1) * cap] = jnp.where(
                hit, 1.0, 0.0
            ).astype(jnp.bfloat16)

    def add_up(q):
        for t in order:
            s = (g - t + groups) % groups
            remote(
                arrived.at[q, s], arrived.at[q, s], sem_vec, (q, t - 1), {"grp": grp_at(t)}
            ).wait_recv()
        keep(arrived.at[q], arr_out.at[q], 1 + q)
        high_rows = min(share, 256)
        for t in [*range(1, inner), 0]:
            xt = (xi + t) % inner

            @pl.loop(0, share // high_rows)
            def _(i):
                start = pl.multiple_of(xt * share + i * high_rows, high_rows)
                total = jnp.dot(
                    member[pl.ds(start, high_rows), :],
                    arrived[q].reshape(slots, cols),
                    preferred_element_type=jnp.float32,
                )
                sums[q, xt, pl.ds(pl.multiple_of(i * high_rows, high_rows), high_rows), :] = total.astype(
                    jnp.bfloat16
                )

            if t:
                send(sums.at[q, xt], x_in.at[q, t - 1], sem_x, (q, t - 1), x_dev(t))

    def over_x(q):
        for t in range(1, inner):
            remote(x_in.at[q, t - 1], x_in.at[q, t - 1], sem_x, (q, t - 1), x_dev(t)).wait_recv()
        for t in [*range(1, outer), 0]:
            zt = (zi + t) % outer
            span = pl.ds(pl.multiple_of(zt * part, part), part)
            total = sums[q, xi, span, :].astype(jnp.float32)
            for u in range(inner - 1):
                total = total + x_in[q, u, span, :].astype(jnp.float32)
            half[q, zt] = total.astype(jnp.bfloat16)
            if t:
                send(half.at[q, zt], z_in.at[q, t - 1], sem_z, (q, t - 1), z_dev(t))

    def codes_over_x():
        for t in range(1, inner):
            remote(group_codes.at[0, t], group_codes.at[0, t], sem_xcode, (t - 1,), x_dev(t)).wait_recv()
        for t in range(1, outer):
            send(group_codes.at[0], group_codes.at[t], sem_zcode, (t - 1,), z_dev(t))

    def count_children():
        for t in range(1, outer):
            remote(group_codes.at[t], group_codes.at[t], sem_zcode, (t - 1,), z_dev(t)).wait_recv()
        ids = lax.broadcasted_iota(jnp.int32, (part, 128), 0) + (xi * outer + zi) * part

        def one_member(i, running):
            block = group_codes.at[i // inner, i % inner]
            for s in range(groups):
                for lane in range(0, cap, 128):
                    hit = ids == block[s : s + 1, lane : lane + 128]
                    running = running + jnp.where(hit, 1.0, 0.0)
            return running

        tally = lax.fori_loop(0, inner * outer, one_member, jnp.zeros((part, 128), jnp.float32))
        return jnp.maximum(jnp.sum(tally, axis=1, keepdims=True), 1.0)

    def over_z(q, tally):
        for t in range(1, outer):
            remote(z_in.at[q, t - 1], z_in.at[q, t - 1], sem_z, (q, t - 1), z_dev(t)).wait_recv()
        total = half[q, zi].astype(jnp.float32)
        for u in range(outer - 1):
            total = total + z_in[q, u].astype(jnp.float32)
        cent[q, xi, zi] = (total / tally).astype(jnp.bfloat16)
        for t in range(1, outer):
            send(cent.at[q, xi, zi], cent.at[q, xi, zi], sem_zc, (q, t - 1), z_dev(t))

    def back_over_z(q):
        for t in range(1, outer):
            zs = (zi - t + outer) % outer
            remote(cent.at[q, xi, zs], cent.at[q, xi, zs], sem_zc, (q, t - 1), z_dev(t)).wait_recv()
        for t in range(1, inner):
            send(cent.at[q, xi], cent.at[q, xi], sem_xc, (q, t - 1), x_dev(t))

    def back_over_x(q):
        for t in range(1, inner):
            xs = (xi - t + inner) % inner
            remote(cent.at[q, xs], cent.at[q, xs], sem_xc, (q, t - 1), x_dev(t)).wait_recv()
        keep(cent.at[q], cent_out.at[q], 1 + blocks + q)

    tally = None
    for beat in range(blocks + 4):
        if beat < blocks:
            add_up(beat)
        if beat == 0:
            codes_over_x()
        if 0 <= beat - 1 < blocks:
            over_x(beat - 1)
        if beat == 1:
            tally = count_children()
        if 0 <= beat - 2 < blocks:
            over_z(beat - 2, tally)
        if 0 <= beat - 3 < blocks:
            back_over_z(beat - 3)
        if 0 <= beat - 4 < blocks:
            back_over_x(beat - 4)

    for copy in kept:
        copy.wait()
    for copy in sent:
        copy.wait_send()


def distance_kernel(depth, arr_ref, cent_ref, code_ref, out_ref, norms):
    blocks = cent_ref.shape[0]

    @pl.when(pl.program_id(0) == 0)
    def _():
        for base in range(0, WIDTH, 128):
            square = jnp.zeros((128, 128), jnp.float32)
            for q in range(blocks):
                wide = cent_ref[q, base : base + 128, :].astype(jnp.float32)
                wide = wide * wide
                for lane in range(0, wide.shape[1], 128):
                    square = square + wide[:, lane : lane + 128]
            norms[:, base : base + 128] = jnp.broadcast_to(
                jnp.sum(square.T, axis=0, keepdims=True), (8, 128)
            )

    rows = arr_ref.shape[1]
    mark = pl.program_id(0)
    lanes = lax.broadcasted_iota(jnp.int32, code_ref.shape, 0)
    row_codes = jnp.sum(jnp.where(lanes == mark, code_ref[...], 0), axis=0, keepdims=True)
    column = jnp.broadcast_to(row_codes.astype(jnp.float32), (128, rows)).T[:, 0:1]
    x = jnp.concatenate([arr_ref[q] for q in range(blocks)], axis=1)
    wide = x.astype(jnp.float32)
    x_norm = jnp.sum(wide * wide, axis=1, keepdims=True)
    second = column >= CHILD
    filled = column >= 0
    step = 256
    for base in range(0, CHILD, step):
        values = []
        for p in range(PAR_GRP):
            start = p * CHILD + base
            c = jnp.concatenate([cent_ref[q, start : start + step, :] for q in range(blocks)], axis=1)
            cross = lax.dot_general(x, c, (((1,), (1,)), ((), ())), preferred_element_type=jnp.float32)
            values.append(norms[0:1, start : start + step] - 2.0 * cross)
        dist = (x_norm + jnp.where(second, values[1], values[0])) * (1.0 / depth)
        out_ref[:, base : base + step] = jnp.where(filled, dist, 0.0)


def body(vectors, parents, children, counts):
    groups = lax.axis_size("grp")
    members = lax.axis_size("mem")
    inner = inner_size(members)
    outer = members // inner
    rows, depth = vectors.shape
    cap = 2 * rows // groups
    slots = groups * cap
    cols = 256
    blocks = depth // cols
    share = WIDTH // inner
    part = share // outer
    code_high = max(8, groups)
    bf16, i32 = jnp.bfloat16, jnp.int32
    dims = (groups, inner, outer, rows, cap, blocks, cols)
    vmem = pltpu.VMEM
    dma = pltpu.SemaphoreType.DMA
    arr, cent, codes = pl.pallas_call(
        functools.partial(exchange_kernel, dims),
        out_shape=(
            jax.ShapeDtypeStruct((blocks, groups, cap, cols), bf16),
            jax.ShapeDtypeStruct((blocks, inner, outer, part, cols), bf16),
            jax.ShapeDtypeStruct((code_high, cap), i32),
        ),
        in_specs=[
            pl.BlockSpec(memory_space=pltpu.SMEM),
            pl.BlockSpec(memory_space=vmem),
            pl.BlockSpec(memory_space=vmem),
            pl.BlockSpec(memory_space=vmem),
        ],
        out_specs=(pl.BlockSpec(memory_space=pl.ANY),) * 3,
        scratch_shapes=[
            vmem((groups, cap, rows), bf16),
            vmem((groups - 1, 8, cap), i32),
            vmem((groups, 8, cap), i32),
            vmem((outer, inner, code_high, cap), i32),
            vmem((blocks, groups - 1, cap, cols), bf16),
            vmem((blocks, groups, cap, cols), bf16),
            vmem((WIDTH, slots), bf16),
            vmem((blocks, inner, share, cols), bf16),
            vmem((blocks, inner - 1, share, cols), bf16),
            vmem((blocks, outer, part, cols), bf16),
            vmem((blocks, outer - 1, part, cols), bf16),
            vmem((blocks, inner, outer, part, cols), bf16),
            dma((2, groups - 1)),
            dma((2, blocks, groups - 1)),
            dma((2, inner - 1)),
            dma((2, outer - 1)),
            dma((2, blocks, inner - 1)),
            dma((2, blocks, outer - 1)),
            dma((2, blocks, outer - 1)),
            dma((2, blocks, inner - 1)),
            dma((1 + 2 * blocks,)),
        ],
        compiler_params=pltpu.CompilerParams(
            collective_id=0, has_side_effects=True, vmem_limit_bytes=56 * MIB
        ),
    )(counts, vectors, parents.reshape(1, rows), children.reshape(1, rows))
    arr = arr.reshape(blocks, slots, cols)
    cent = cent.reshape(blocks, WIDTH, cols)
    return pl.pallas_call(
        functools.partial(distance_kernel, depth),
        grid=(groups,),
        out_shape=jax.ShapeDtypeStruct((slots, CHILD), jnp.float32),
        in_specs=[
            pl.BlockSpec((blocks, cap, cols), lambda i: (0, i, 0)),
            pl.BlockSpec((blocks, WIDTH, cols), lambda i: (0, 0, 0)),
            pl.BlockSpec((code_high, cap), lambda i: (0, 0)),
        ],
        out_specs=pl.BlockSpec((cap, CHILD), lambda i: (i, 0)),
        scratch_shapes=[vmem((8, WIDTH), jnp.float32)],
        compiler_params=pltpu.CompilerParams(vmem_limit_bytes=48 * MIB),
    )(arr, cent, codes)


def solution(mesh):
    in_specs = (
        P(("grp", "mem"), None),
        P(("grp", "mem")),
        P(("grp", "mem")),
        P(("grp", "mem"), None),
    )
    out_specs = P(("grp", "mem"), None)
    return jax.shard_map(body, mesh=mesh, in_specs=in_specs, out_specs=out_specs, check_vma=False)
```

time: 298 us -> 138 us (0.46); the launches traced: 294 us -> 137 us
  waiting for transfers between devices: 142 us -> 0 us
  Pallas kernels: 0 us -> 135 us
  matrix products: 41.5 us -> 0 us
  local copies, waits for them, and re-layouts: 37.5 us -> 2.6 us
  other arithmetic: 31.6 us -> 0 us
  blocking collectives: 19.6 us -> 0 us
  between operations: 13.6 us -> 0.02 us
  starting transfers between devices: 8.38 us -> 0 us
    pallas_call x0 -> x2, Pallas kernels: none -> 135 us  [the longest x1 123 us: body(): pl.pallas_call(functools.partial(exchange_kernel, dims), out_shape=(jax.S...]
    psum x1 -> x0, waiting for transfers between devices: 107 us -> none  [body(): lax.psum(child_sums.astype(jnp.bfloat16), 'mem').astype(jnp.float32)]
    dot_general x5 -> x0, matrix products: 41.5 us -> none  [the longest x4 28.8 us: add_into_totals(): lax.dot_general(onehot, block_vecs, (((0,), (0,)), ((), ())), preferred_e...]
    all_to_all x2 -> x0, waiting for transfers between devices: 35.3 us -> none  [the longest x1 35.3 us: body(): lax.all_to_all(outgoing_rows, 'grp', split_axis=0, concat_axis=0, tiled=T...]
    gather x3 -> x0, local copies, waits for them, and re-layouts: 28.2 us -> none  [the longest x1 10.2 us: body(): jnp.take(children, source_rows)]
    psum x1 -> x0, blocking collectives: 19.6 us -> none  [body(): lax.psum(child_counts.astype(jnp.bfloat16), 'mem').astype(jnp.float32)]
    reduce_sum x7 -> x0, other arithmetic: 15.4 us -> none  [the longest x1 8.04 us: pick_parent(): jnp.sum(jnp.where(chosen, stacked, jnp.zeros((), jnp.float32)), axis=1)]
    select_n x1 -> x0, local copies, waits for them, and re-layouts: 9.24 us -> none  [pick_parent(): jnp.where(row_codes[:, None] >= 0, picked, jnp.zeros((), jnp.float32))]
  transfers between devices with their start and end apart: 3 -> 0, of which waited for: 2 -> 0; matrix products, arithmetic and copies ran while one was open for 5% -> 0% of each run, Pallas kernels for 0% -> 0%
where the time goes in v1:
time: 138 us; the launch traced here: 137 us
  Pallas kernels  135 us (98%)
  local copies, waits for them, and re-layouts  2.6 us (2%)
    pallas_call x1, Pallas kernels, body(): pl.pallas_call(functools.partial(exchange_kernel, dims), out_shape=(jax.S...  123 us
    pallas_call x1, Pallas kernels, body(): pl.pallas_call(functools.partial(distance_kernel, depth), grid=(groups,),...  12.2 us

profile of v1, /device:TPU:12, one launch (start us, length us, event | category | flops | bytes accessed | tf_op | source)
XLA Modules:
  0.0 137.4 jit_solution(884192310206073093)
XLA Ops:
  0.0 122.6 %shard_map.46 = (bf16[3,4,512,256]{3,2,1,0:T(8,128)(2,1)}, bf16[3,2,4,256,256]{4,3,2,1,0:T(8,128)(2,1)}, s32[8,512]{1,0:T(8,128)}) custom-call(s32[1,4]{1,0:T(1,128)} %counts_ref.1, bf16[1024,768]{1,0:T(8,128)(2,1)} %vec_ref.1, s32[1,1024]{1,0:T(1,128)} %bitcast.6, s32[1,1024]{1,0:T(1,128)} %bitcast.7), custom_call_target="tpu_custom_call" | custom-call | tf_op jit(solution)/shard_map/pallas_call | solution.py:333
  122.6 0.0 copy-start
  122.6 1.9 %copy-done = bf16[3,4,512,256]{3,2,1,0:T(8,128)(2,1)S(1)} copy-done((bf16[3,4,512,256]{3,2,1,0:T(8,128)(2,1)S(1)}, bf16[3,4,512,256]{3,2,1,0:T(8,128)(2,1)}, u32[]{:S(2)}) %copy-start) | copy-done | bytes 3145752
  124.5 0.0 copy-start.1
  124.5 0.7 copy-done.1
  125.2 12.2 %shard_map.47 = f32[2048,1024]{1,0:T(8,128)} custom-call(bf16[3,2048,256]{2,1,0:T(8,128)(2,1)S(1)} %bitcast.4, bf16[3,2048,256]{2,1,0:T(8,128)(2,1)} %bitcast.5, s32[8,512]{1,0:T(8,128)S(1)} %copy-done.1), custom_call_target="tpu_custom_call" | custom-call | tf_op jit(solution)/shard_map/pallas_call | solution.py:376
Async XLA Ops:
  122.6 1.9 %copy-start = (bf16[3,4,512,256]{3,2,1,0:T(8,128)(2,1)S(1)}, bf16[3,4,512,256]{3,2,1,0:T(8,128)(2,1)}, u32[]{:S(2)}) copy-start(bf16[3,4,512,256]{3,2,1,0:T(8,128)(2,1)} %get-tuple-element.8) | copy-start | bytes 9437188
  124.5 0.7 copy-start.1

commit v2 on v1

--- a/solution.py
+++ b/solution.py
@@ -12,6 +12,7 @@
 WIDTH = PAR_GRP * CHILD
 LOW = 32
 MIB = 1024 * 1024
+PIECES = 2
 
 
 def inner_size(members):
@@ -27,6 +28,7 @@
     arr_out,
     cent_out,
     code_out,
+    norm_out,
     pick,
     out_codes,
     in_codes,
@@ -39,6 +41,8 @@
     half,
     z_in,
     cent,
+    squares,
+    norms,
     sem_code,
     sem_vec,
     sem_xcode,
@@ -52,7 +56,8 @@
     groups, inner, outer, rows, cap, blocks, cols = dims
     slots = groups * cap
     share = WIDTH // inner
-    part = share // outer
+    tall = share // PIECES
+    part = tall // outer
     g = lax.axis_index("grp")
     m = lax.axis_index("mem")
     zi, xi = m // inner, m % inner
@@ -157,55 +162,46 @@
         send(group_codes.at[0, 0], group_codes.at[0, t], sem_xcode, (t - 1,), x_dev(t))
     keep(group_codes.at[0, 0], code_out, 0)
 
-    tall = 256
-
-    @pl.loop(0, WIDTH // tall)
+    @pl.loop(0, WIDTH // 256)
     def _(i):
-        ids = lax.broadcasted_iota(jnp.int32, (tall, cap), 0) + i * tall
+        ids = lax.broadcasted_iota(jnp.int32, (256, cap), 0) + i * 256
         for s in range(groups):
             hit = ids == in_codes[s, 0:1, :]
-            member[pl.ds(pl.multiple_of(i * tall, tall), tall), s * cap : (s + 1) * cap] = jnp.where(
+            member[pl.ds(pl.multiple_of(i * 256, 256), 256), s * cap : (s + 1) * cap] = jnp.where(
                 hit, 1.0, 0.0
             ).astype(jnp.bfloat16)
 
-    def add_up(q):
-        for t in order:
-            s = (g - t + groups) % groups
-            remote(
-                arrived.at[q, s], arrived.at[q, s], sem_vec, (q, t - 1), {"grp": grp_at(t)}
-            ).wait_recv()
-        keep(arrived.at[q], arr_out.at[q], 1 + q)
-        high_rows = min(share, 256)
+    def add_up(q, r):
+        if r == 0:
+            for t in order:
+                s = (g - t + groups) % groups
+                remote(
+                    arrived.at[q, s], arrived.at[q, s], sem_vec, (q, t - 1), {"grp": grp_at(t)}
+                ).wait_recv()
+            keep(arrived.at[q], arr_out.at[q], 2 + q)
         for t in [*range(1, inner), 0]:
             xt = (xi + t) % inner
-
-            @pl.loop(0, share // high_rows)
-            def _(i):
-                start = pl.multiple_of(xt * share + i * high_rows, high_rows)
-                total = jnp.dot(
-                    member[pl.ds(start, high_rows), :],
-                    arrived[q].reshape(slots, cols),
-                    preferred_element_type=jnp.float32,
-                )
-                sums[q, xt, pl.ds(pl.multiple_of(i * high_rows, high_rows), high_rows), :] = total.astype(
-                    jnp.bfloat16
-                )
-
+            total = jnp.dot(
+                member[pl.ds(pl.multiple_of(xt * share + r * tall, tall), tall), :],
+                arrived[q].reshape(slots, cols),
+                preferred_element_type=jnp.float32,
+            )
+            sums[q, r, xt] = total.astype(jnp.bfloat16)
             if t:
-                send(sums.at[q, xt], x_in.at[q, t - 1], sem_x, (q, t - 1), x_dev(t))
-
-    def over_x(q):
+                send(sums.at[q, r, xt], x_in.at[q, r, t - 1], sem_x, (q, r, t - 1), x_dev(t))
+
+    def over_x(q, r):
         for t in range(1, inner):
-            remote(x_in.at[q, t - 1], x_in.at[q, t - 1], sem_x, (q, t - 1), x_dev(t)).wait_recv()
+            remote(x_in.at[q, r, t - 1], x_in.at[q, r, t - 1], sem_x, (q, r, t - 1), x_dev(t)).wait_recv()
         for t in [*range(1, outer), 0]:
             zt = (zi + t) % outer
             span = pl.ds(pl.multiple_of(zt * part, part), part)
-            total = sums[q, xi, span, :].astype(jnp.float32)
+            total = sums[q, r, xi, span, :].astype(jnp.float32)
             for u in range(inner - 1):
-                total = total + x_in[q, u, span, :].astype(jnp.float32)
-            half[q, zt] = total.astype(jnp.bfloat16)
+                total = total + x_in[q, r, u, span, :].astype(jnp.float32)
+            half[q, r, zt] = total.astype(jnp.bfloat16)
             if t:
-                send(half.at[q, zt], z_in.at[q, t - 1], sem_z, (q, t - 1), z_dev(t))
+                send(half.at[q, r, zt], z_in.at[q, r, t - 1], sem_z, (q, r, t - 1), z_dev(t))
 
     def codes_over_x():
         for t in range(1, inner):
@@ -213,10 +209,12 @@
         for t in range(1, outer):
             send(group_codes.at[0], group_codes.at[t], sem_zcode, (t - 1,), z_dev(t))
 
-    def count_children():
+    def codes_over_z():
         for t in range(1, outer):
             remote(group_codes.at[t], group_codes.at[t], sem_zcode, (t - 1,), z_dev(t)).wait_recv()
-        ids = lax.broadcasted_iota(jnp.int32, (part, 128), 0) + (xi * outer + zi) * part
+
+    def count_children(r):
+        ids = lax.broadcasted_iota(jnp.int32, (part, 128), 0) + ((xi * PIECES + r) * outer + zi) * part
 
         def one_member(i, running):
             block = group_codes.at[i // inner, i % inner]
@@ -229,87 +227,98 @@
         tally = lax.fori_loop(0, inner * outer, one_member, jnp.zeros((part, 128), jnp.float32))
         return jnp.maximum(jnp.sum(tally, axis=1, keepdims=True), 1.0)
 
-    def over_z(q, tally):
+    def over_z(q, r):
         for t in range(1, outer):
-            remote(z_in.at[q, t - 1], z_in.at[q, t - 1], sem_z, (q, t - 1), z_dev(t)).wait_recv()
-        total = half[q, zi].astype(jnp.float32)
+            remote(z_in.at[q, r, t - 1], z_in.at[q, r, t - 1], sem_z, (q, r, t - 1), z_dev(t)).wait_recv()
+        total = half[q, r, zi].astype(jnp.float32)
         for u in range(outer - 1):
-            total = total + z_in[q, u].astype(jnp.float32)
-        cent[q, xi, zi] = (total / tally).astype(jnp.bfloat16)
+            total = total + z_in[q, r, u].astype(jnp.float32)
+        cent[q, xi, r, zi] = (total / tallies[r]).astype(jnp.bfloat16)
+        block = cent.at[q, xi, r, zi]
         for t in range(1, outer):
-            send(cent.at[q, xi, zi], cent.at[q, xi, zi], sem_zc, (q, t - 1), z_dev(t))
-
-    def back_over_z(q):
+            send(block, block, sem_zc, (q, r, t - 1), z_dev(t))
+        for t in range(1, inner):
+            send(block, block, sem_xc, (q, r, 0, t - 1), x_dev(t))
+
+    def back_over_z(q, r):
         for t in range(1, outer):
-            zs = (zi - t + outer) % outer
-            remote(cent.at[q, xi, zs], cent.at[q, xi, zs], sem_zc, (q, t - 1), z_dev(t)).wait_recv()
-        for t in range(1, inner):
-            send(cent.at[q, xi], cent.at[q, xi], sem_xc, (q, t - 1), x_dev(t))
-
-    def back_over_x(q):
-        for t in range(1, inner):
-            xs = (xi - t + inner) % inner
-            remote(cent.at[q, xs], cent.at[q, xs], sem_xc, (q, t - 1), x_dev(t)).wait_recv()
-        keep(cent.at[q], cent_out.at[q], 1 + blocks + q)
-
-    tally = None
-    for beat in range(blocks + 4):
-        if beat < blocks:
-            add_up(beat)
-        if beat == 0:
-            codes_over_x()
-        if 0 <= beat - 1 < blocks:
-            over_x(beat - 1)
-        if beat == 1:
-            tally = count_children()
-        if 0 <= beat - 2 < blocks:
-            over_z(beat - 2, tally)
-        if 0 <= beat - 3 < blocks:
-            back_over_z(beat - 3)
-        if 0 <= beat - 4 < blocks:
-            back_over_x(beat - 4)
-
+            block = cent.at[q, xi, r, (zi - t + outer) % outer]
+            remote(block, block, sem_zc, (q, r, t - 1), z_dev(t)).wait_recv()
+            for u in range(1, inner):
+                send(block, block, sem_xc, (q, r, t, u - 1), x_dev(u))
+
+    def back_over_x(q, r):
+        for t in range(outer):
+            for u in range(1, inner):
+                block = cent.at[q, (xi - u + inner) % inner, r, (zi - t + outer) % outer]
+                remote(block, block, sem_xc, (q, r, t, u - 1), x_dev(u)).wait_recv()
+        for x in range(inner):
+            keep(cent.at[q, x, r], cent_out.at[q, x, r], 2 + blocks + (q * PIECES + r) * inner + x)
+        for x in range(inner):
+            for base in range(0, tall, 128):
+                wide = cent[q, x, r].reshape(tall, cols)[base : base + 128].astype(jnp.float32)
+                wide = wide * wide
+                square = wide[:, 0:128]
+                for lane in range(128, cols, 128):
+                    square = square + wide[:, lane : lane + 128]
+                child = (x * PIECES + r) * tall + base
+                if q > 0:
+                    square = square + squares[child : child + 128, :]
+                if q < blocks - 1:
+                    squares[child : child + 128, :] = square
+                else:
+                    norms[:, child : child + 128] = jnp.broadcast_to(
+                        jnp.sum(square.T, axis=0, keepdims=True), (8, 128)
+                    )
+
+    tasks = []
+    for q in range(blocks):
+        for r in range(PIECES):
+            sum_at = 22.0 * q + r
+            x_at = 22.0 * q + 12.0 + 11.0 * r
+            stages = (add_up, over_x, over_z, back_over_z, back_over_x)
+            for number, stage in enumerate(stages):
+                when = sum_at if number == 0 else x_at + 12.0 * (number - 1)
+                tasks.append((when / 2.0, number, stage, (q, r)))
+    tasks.append((1.5, 9, codes_over_x, ()))
+    tasks.append((8.5, 9, codes_over_z, ()))
+    tallies = []
+    for r in range(PIECES):
+        tasks.append((8.6 + r / 10, 9, lambda number: tallies.append(count_children(number)), (r,)))
+    for when, number, stage, where in sorted(tasks, key=lambda task: task[:2]):
+        stage(*where)
+
+    keep(norms, norm_out, 1)
     for copy in kept:
         copy.wait()
     for copy in sent:
         copy.wait_send()
 
 
-def distance_kernel(depth, arr_ref, cent_ref, code_ref, out_ref, norms):
-    blocks = cent_ref.shape[0]
-
-    @pl.when(pl.program_id(0) == 0)
-    def _():
-        for base in range(0, WIDTH, 128):
-            square = jnp.zeros((128, 128), jnp.float32)
-            for q in range(blocks):
-                wide = cent_ref[q, base : base + 128, :].astype(jnp.float32)
-                wide = wide * wide
-                for lane in range(0, wide.shape[1], 128):
-                    square = square + wide[:, lane : lane + 128]
-            norms[:, base : base + 128] = jnp.broadcast_to(
-                jnp.sum(square.T, axis=0, keepdims=True), (8, 128)
-            )
-
-    rows = arr_ref.shape[1]
+def distance_kernel(depth, arr_ref, cent_ref, code_ref, norm_ref, out_ref):
+    blocks, rows = arr_ref.shape[:2]
     mark = pl.program_id(0)
     lanes = lax.broadcasted_iota(jnp.int32, code_ref.shape, 0)
     row_codes = jnp.sum(jnp.where(lanes == mark, code_ref[...], 0), axis=0, keepdims=True)
     column = jnp.broadcast_to(row_codes.astype(jnp.float32), (128, rows)).T[:, 0:1]
     x = jnp.concatenate([arr_ref[q] for q in range(blocks)], axis=1)
     wide = x.astype(jnp.float32)
-    x_norm = jnp.sum(wide * wide, axis=1, keepdims=True)
     second = column >= CHILD
     filled = column >= 0
+    x_norm = jnp.sum(wide * wide, axis=1, keepdims=True) * (1.0 / depth)
     step = 256
     for base in range(0, CHILD, step):
-        values = []
+        crosses, squares = [], []
         for p in range(PAR_GRP):
             start = p * CHILD + base
             c = jnp.concatenate([cent_ref[q, start : start + step, :] for q in range(blocks)], axis=1)
-            cross = lax.dot_general(x, c, (((1,), (1,)), ((), ())), preferred_element_type=jnp.float32)
-            values.append(norms[0:1, start : start + step] - 2.0 * cross)
-        dist = (x_norm + jnp.where(second, values[1], values[0])) * (1.0 / depth)
+            crosses.append(
+                lax.dot_general(x, c, (((1,), (1,)), ((), ())), preferred_element_type=jnp.float32)
+            )
+            squares.append(norm_ref[0:1, start : start + step] * (1.0 / depth))
+        cross = jnp.where(second, crosses[1], crosses[0])
+        square = jnp.where(second, squares[1], squares[0])
+        dist = (x_norm + square) - cross * (2.0 / depth)
         out_ref[:, base : base + step] = jnp.where(filled, dist, 0.0)
 
 
@@ -324,18 +333,20 @@
     cols = 256
     blocks = depth // cols
     share = WIDTH // inner
-    part = share // outer
+    tall = share // PIECES
+    part = tall // outer
     code_high = max(8, groups)
     bf16, i32 = jnp.bfloat16, jnp.int32
     dims = (groups, inner, outer, rows, cap, blocks, cols)
     vmem = pltpu.VMEM
     dma = pltpu.SemaphoreType.DMA
-    arr, cent, codes = pl.pallas_call(
+    arr, cent, codes, norms = pl.pallas_call(
         functools.partial(exchange_kernel, dims),
         out_shape=(
             jax.ShapeDtypeStruct((blocks, groups, cap, cols), bf16),
-            jax.ShapeDtypeStruct((blocks, inner, outer, part, cols), bf16),
+            jax.ShapeDtypeStruct((blocks, inner, PIECES, outer, part, cols), bf16),
             jax.ShapeDtypeStruct((code_high, cap), i32),
+            jax.ShapeDtypeStruct((8, WIDTH), jnp.float32),
         ),
         in_specs=[
             pl.BlockSpec(memory_space=pltpu.SMEM),
@@ -343,7 +354,7 @@
             pl.BlockSpec(memory_space=vmem),
             pl.BlockSpec(memory_space=vmem),
         ],
-        out_specs=(pl.BlockSpec(memory_space=pl.ANY),) * 3,
+        out_specs=(pl.BlockSpec(memory_space=pl.ANY),) * 4,
         scratch_shapes=[
             vmem((groups, cap, rows), bf16),
             vmem((groups - 1, 8, cap), i32),
@@ -352,20 +363,22 @@
             vmem((blocks, groups - 1, cap, cols), bf16),
             vmem((blocks, groups, cap, cols), bf16),
             vmem((WIDTH, slots), bf16),
-            vmem((blocks, inner, share, cols), bf16),
-            vmem((blocks, inner - 1, share, cols), bf16),
-            vmem((blocks, outer, part, cols), bf16),
-            vmem((blocks, outer - 1, part, cols), bf16),
-            vmem((blocks, inner, outer, part, cols), bf16),
+            vmem((blocks, PIECES, inner, tall, cols), bf16),
+            vmem((blocks, PIECES, inner - 1, tall, cols), bf16),
+            vmem((blocks, PIECES, outer, part, cols), bf16),
+            vmem((blocks, PIECES, outer - 1, part, cols), bf16),
+            vmem((blocks, inner, PIECES, outer, part, cols), bf16),
+            vmem((WIDTH, 128), jnp.float32),
+            vmem((8, WIDTH), jnp.float32),
             dma((2, groups - 1)),
             dma((2, blocks, groups - 1)),
             dma((2, inner - 1)),
             dma((2, outer - 1)),
-            dma((2, blocks, inner - 1)),
-            dma((2, blocks, outer - 1)),
-            dma((2, blocks, outer - 1)),
-            dma((2, blocks, inner - 1)),
-            dma((1 + 2 * blocks,)),
+            dma((2, blocks, PIECES, inner - 1)),
+            dma((2, blocks, PIECES, outer - 1)),
+            dma((2, blocks, PIECES, outer - 1)),
+            dma((2, blocks, PIECES, outer, inner - 1)),
+            dma((2 + blocks + blocks * PIECES * inner,)),
         ],
         compiler_params=pltpu.CompilerParams(
             collective_id=0, has_side_effects=True, vmem_limit_bytes=56 * MIB
@@ -381,11 +394,11 @@
             pl.BlockSpec((blocks, cap, cols), lambda i: (0, i, 0)),
             pl.BlockSpec((blocks, WIDTH, cols), lambda i: (0, 0, 0)),
             pl.BlockSpec((code_high, cap), lambda i: (0, 0)),
+            pl.BlockSpec((8, WIDTH), lambda i: (0, 0)),
         ],
         out_specs=pl.BlockSpec((cap, CHILD), lambda i: (i, 0)),
-        scratch_shapes=[vmem((8, WIDTH), jnp.float32)],
-        compiler_params=pltpu.CompilerParams(vmem_limit_bytes=48 * MIB),
-    )(arr, cent, codes)
+        compiler_params=pltpu.CompilerParams(vmem_limit_bytes=60 * MIB),
+    )(arr, cent, codes, norms)
 
 
 def solution(mesh):

time: 138 us -> 116 us (0.84)
  the two profiles are of different devices: /device:TPU:12 before, /device:TPU:25 now
where the time goes in v2:
time: 116 us
  Pallas kernels  116 us (100%)
    pallas_call x1, Pallas kernels, body(): pl.pallas_call(functools.partial(exchange_kernel, dims), out_shape=(jax.S...  105 us
    pallas_call x1, Pallas kernels, body(): pl.pallas_call(functools.partial(distance_kernel, depth), grid=(groups,),...  11.3 us

profile of v2, /device:TPU:25, one launch (start us, length us, event | category | flops | bytes accessed | tf_op | source)
XLA Modules:
  0.0 116.0 jit_solution(56234260832051226)
XLA Ops:
  0.0 104.7 %shard_map.46 = (bf16[3,4,512,256]{3,2,1,0:T(8,128)(2,1)}, bf16[3,2,2,4,128,256]{5,4,3,2,1,0:T(8,128)(2,1)}, s32[8,512]{1,0:T(8,128)}, f32[8,2048]{1,0:T(8,128)}) custom-call(s32[1,4]{1,0:T(1,128)} %counts_ref.1, bf16[1024,768]{1,0:T(8,128)(2,1)} %vec_ref.1, s32[1,1024]{1,0:T(1,128)} %bitcast.6, s32[1,1024]{1,0:T(1,128)} %bitcast.7), custom_call_target="tpu_custom_call" | custom-call | tf_op jit(solution)/shard_map/pallas_call | solution.py:343
  104.7 11.3 %shard_map.47 = f32[2048,1024]{1,0:T(8,128)} custom-call(bf16[3,2048,256]{2,1,0:T(8,128)(2,1)} %bitcast.4, bf16[3,2048,256]{2,1,0:T(8,128)(2,1)} %bitcast.5, s32[8,512]{1,0:T(8,128)} %get-tuple-element.11.code_ref, f32[8,2048]{1,0:T(8,128)} %get-tuple-element.12.norm_ref), custom_call_target="tpu_custom_call" | custom-call | tf_op jit(solution)/shard_map/pallas_call | solution.py:389

commit v3 on v2

--- a/solution.py
+++ b/solution.py
@@ -12,7 +12,7 @@
 WIDTH = PAR_GRP * CHILD
 LOW = 32
 MIB = 1024 * 1024
-PIECES = 2
+PIECES = 1
 
 
 def inner_size(members):
@@ -126,29 +126,43 @@
         value = (got[0:1] * LOW + got[1:2] - LOW).astype(jnp.int32)
         return jnp.broadcast_to(value, (8, cap))
 
-    def picked(t, q):
-        return jnp.dot(
-            pick[t], vec_ref[:, q * cols : (q + 1) * cols], preferred_element_type=jnp.float32
-        ).astype(jnp.bfloat16)
-
-    def send_rows(t, q):
-        outgoing[q, t - 1] = picked(t, q)
-        send(outgoing.at[q, t - 1], arrived.at[q, g], sem_vec, (q, t - 1), {"grp": grp_at(t)})
+    batches = [(0,), (1,)] + [tuple(range(q, min(q + 2, blocks))) for q in range(2, blocks, 2)]
+
+    def pick_rows(t, batch):
+        rows_of = vec_ref[:, batch[0] * cols : (batch[-1] + 1) * cols]
+        found = jnp.dot(pick[t], rows_of, preferred_element_type=jnp.float32).astype(jnp.bfloat16)
+        for place, q in enumerate(batch):
+            block = found[:, place * cols : (place + 1) * cols]
+            if t:
+                outgoing[q, t - 1] = block
+            else:
+                arrived[q, g] = block
+
+    def send_rows(t, batch):
+        for q in batch:
+            send(outgoing.at[q, t - 1], arrived.at[q, g], sem_vec, (q, t - 1), {"grp": grp_at(t)})
 
     order = sorted(range(1, groups), key=lambda t: abs(2 * t - groups))
     for place, t in enumerate(order):
         out_codes[t - 1] = make_pick(t)
-        outgoing[0, t - 1] = picked(t, 0)
+        pick_rows(t, batches[0])
         if place == 0:
             pl.semaphore_wait(barrier, groups + inner + outer - 3)
         send(out_codes.at[t - 1], in_codes.at[g], sem_code, (t - 1,), {"grp": grp_at(t)})
-        send(outgoing.at[0, t - 1], arrived.at[0, g], sem_vec, (0, t - 1), {"grp": grp_at(t)})
+        send_rows(t, batches[0])
+    for t in order:
+        pick_rows(t, batches[1])
+        send_rows(t, batches[1])
     in_codes[g] = make_pick(0)
-    arrived[0, g] = picked(0, 0)
-    for q in range(1, blocks):
-        for t in order:
-            send_rows(t, q)
-        arrived[q, g] = picked(0, q)
+    pick_rows(0, batches[0])
+
+    def pick_later():
+        for batch in batches[2:]:
+            for t in order:
+                pick_rows(t, batch)
+                send_rows(t, batch)
+        for batch in batches[1:]:
+            pick_rows(0, batch)
 
     for t in order:
         s = (g - t + groups) % groups
@@ -171,24 +185,27 @@
                 hit, 1.0, 0.0
             ).astype(jnp.bfloat16)
 
-    def add_up(q, r):
-        if r == 0:
+    def add_up(*batch):
+        for q in batch:
             for t in order:
                 s = (g - t + groups) % groups
                 remote(
                     arrived.at[q, s], arrived.at[q, s], sem_vec, (q, t - 1), {"grp": grp_at(t)}
                 ).wait_recv()
             keep(arrived.at[q], arr_out.at[q], 2 + q)
+        rows_of = jnp.concatenate([arrived[q].reshape(slots, cols) for q in batch], axis=1)
         for t in [*range(1, inner), 0]:
             xt = (xi + t) % inner
-            total = jnp.dot(
-                member[pl.ds(pl.multiple_of(xt * share + r * tall, tall), tall), :],
-                arrived[q].reshape(slots, cols),
-                preferred_element_type=jnp.float32,
-            )
-            sums[q, r, xt] = total.astype(jnp.bfloat16)
-            if t:
-                send(sums.at[q, r, xt], x_in.at[q, r, t - 1], sem_x, (q, r, t - 1), x_dev(t))
+            for r in range(PIECES):
+                total = jnp.dot(
+                    member[pl.ds(pl.multiple_of(xt * share + r * tall, tall), tall), :],
+                    rows_of,
+                    preferred_element_type=jnp.float32,
+                ).astype(jnp.bfloat16)
+                for place, q in enumerate(batch):
+                    sums[q, r, xt] = total[:, place * cols : (place + 1) * cols]
+                    if t:
+                        send(sums.at[q, r, xt], x_in.at[q, r, t - 1], sem_x, (q, r, t - 1), x_dev(t))
 
     def over_x(q, r):
         for t in range(1, inner):
@@ -240,51 +257,55 @@
         for t in range(1, inner):
             send(block, block, sem_xc, (q, r, 0, t - 1), x_dev(t))
 
+    def add_squares(q, x, r):
+        for base in range(0, tall, 128):
+            wide = cent[q, x, r].reshape(tall, cols)[base : base + 128].astype(jnp.float32)
+            square = wide * wide
+            child = pl.ds(pl.multiple_of((x * PIECES + r) * tall + base, 128), 128)
+            if q > 0:
+                square = square + squares[child, :]
+            if q < blocks - 1:
+                squares[child, :] = square
+            else:
+                norms[:, child] = jnp.broadcast_to(jnp.sum(square.T, axis=0, keepdims=True), (8, 128))
+
+    def write_cent(q, x, r, number):
+        keep(cent.at[q, x, r], cent_out.at[q, x, r], 2 + blocks + (q * PIECES + r) * inner + number)
+
     def back_over_z(q, r):
         for t in range(1, outer):
             block = cent.at[q, xi, r, (zi - t + outer) % outer]
             remote(block, block, sem_zc, (q, r, t - 1), z_dev(t)).wait_recv()
             for u in range(1, inner):
                 send(block, block, sem_xc, (q, r, t, u - 1), x_dev(u))
+        write_cent(q, xi, r, 0)
+        add_squares(q, xi, r)
 
     def back_over_x(q, r):
-        for t in range(outer):
-            for u in range(1, inner):
-                block = cent.at[q, (xi - u + inner) % inner, r, (zi - t + outer) % outer]
+        for u in range(1, inner):
+            x = (xi - u + inner) % inner
+            for t in range(outer):
+                block = cent.at[q, x, r, (zi - t + outer) % outer]
                 remote(block, block, sem_xc, (q, r, t, u - 1), x_dev(u)).wait_recv()
-        for x in range(inner):
-            keep(cent.at[q, x, r], cent_out.at[q, x, r], 2 + blocks + (q * PIECES + r) * inner + x)
-        for x in range(inner):
-            for base in range(0, tall, 128):
-                wide = cent[q, x, r].reshape(tall, cols)[base : base + 128].astype(jnp.float32)
-                wide = wide * wide
-                square = wide[:, 0:128]
-                for lane in range(128, cols, 128):
-                    square = square + wide[:, lane : lane + 128]
-                child = (x * PIECES + r) * tall + base
-                if q > 0:
-                    square = square + squares[child : child + 128, :]
-                if q < blocks - 1:
-                    squares[child : child + 128, :] = square
-                else:
-                    norms[:, child : child + 128] = jnp.broadcast_to(
-                        jnp.sum(square.T, axis=0, keepdims=True), (8, 128)
-                    )
+            write_cent(q, x, r, u)
+            add_squares(q, x, r)
 
     tasks = []
-    for q in range(blocks):
-        for r in range(PIECES):
-            sum_at = 22.0 * q + r
-            x_at = 22.0 * q + 12.0 + 11.0 * r
-            stages = (add_up, over_x, over_z, back_over_z, back_over_x)
-            for number, stage in enumerate(stages):
-                when = sum_at if number == 0 else x_at + 12.0 * (number - 1)
-                tasks.append((when / 2.0, number, stage, (q, r)))
-    tasks.append((1.5, 9, codes_over_x, ()))
-    tasks.append((8.5, 9, codes_over_z, ()))
+    free = 0.0
+    for number, batch in enumerate(batches):
+        ready = 7.0 * batch[-1]
+        tasks.append((ready, 0, add_up, batch))
+        for q in batch:
+            free = max(free, ready + 1.0) + 7.0
+            for r in range(PIECES):
+                for number, stage in enumerate((over_x, over_z, back_over_z, back_over_x)):
+                    tasks.append((free + 7.0 * number, number + 1, stage, (q, r)))
+    tasks.append((0.5, 8, codes_over_x, ()))
+    tasks.append((9.2, 8, codes_over_z, ()))
     tallies = []
     for r in range(PIECES):
-        tasks.append((8.6 + r / 10, 9, lambda number: tallies.append(count_children(number)), (r,)))
+        tasks.append((9.3, 9, lambda number: tallies.append(count_children(number)), (r,)))
+    pick_later()
     for when, number, stage, where in sorted(tasks, key=lambda task: task[:2]):
         stage(*where)
 
@@ -330,7 +351,7 @@
     rows, depth = vectors.shape
     cap = 2 * rows // groups
     slots = groups * cap
-    cols = 256
+    cols = 128
     blocks = depth // cols
     share = WIDTH // inner
     tall = share // PIECES

time: 116 us -> 120 us (1.034)
  the two profiles are of different devices: /device:TPU:25 before, /device:TPU:12 now
where the time goes in v3:
time: 120 us; the launch traced here: 118 us
  Pallas kernels  118 us (98%)
    pallas_call x1, Pallas kernels, body(): pl.pallas_call(functools.partial(exchange_kernel, dims), out_shape=(jax.S...  107 us
    pallas_call x1, Pallas kernels, body(): pl.pallas_call(functools.partial(distance_kernel, depth), grid=(groups,),...  11.2 us

profile of v3, /device:TPU:12, one launch (start us, length us, event | category | flops | bytes accessed | tf_op | source)
XLA Modules:
  0.0 117.8 jit_solution(13549885998346725819)
XLA Ops:
  0.0 106.6 %shard_map.46 = (bf16[6,4,512,128]{3,2,1,0:T(8,128)(2,1)}, bf16[6,2,1,4,256,128]{5,4,3,2,1,0:T(8,128)(2,1)}, s32[8,512]{1,0:T(8,128)}, f32[8,2048]{1,0:T(8,128)}) custom-call(s32[1,4]{1,0:T(1,128)} %counts_ref.1, bf16[1024,768]{1,0:T(8,128)(2,1)} %vec_ref.1, s32[1,1024]{1,0:T(1,128)} %bitcast.6, s32[1,1024]{1,0:T(1,128)} %bitcast.7), custom_call_target="tpu_custom_call" | custom-call | tf_op jit(solution)/shard_map/pallas_call | solution.py:364
  106.6 11.2 %shard_map.47 = f32[2048,1024]{1,0:T(8,128)} custom-call(bf16[6,2048,128]{2,1,0:T(8,128)(2,1)} %bitcast.4, bf16[6,2048,128]{2,1,0:T(8,128)(2,1)} %bitcast.5, s32[8,512]{1,0:T(8,128)} %get-tuple-element.11.code_ref, f32[8,2048]{1,0:T(8,128)} %get-tuple-element.12.norm_ref), custom_call_target="tpu_custom_call" | custom-call | tf_op jit(solution)/shard_map/pallas_call | solution.py:410

commit v4 on v2

--- a/solution.py
+++ b/solution.py
@@ -39,7 +39,9 @@
     sums,
     x_in,
     half,
-    z_in,
+    z_near,
+    pair,
+    z_far,
     cent,
     squares,
     norms,
@@ -61,6 +63,12 @@
     g = lax.axis_index("grp")
     m = lax.axis_index("mem")
     zi, xi = m // inner, m % inner
+    duos = outer // 2
+    side, duo = zi % 2, zi // 2
+    next_z = zi + 1 - 2 * side
+
+    def far_z(t):
+        return 2 * ((duo + t) % duos) + side
 
     def grp_at(t):
         return (g + t) % groups
@@ -70,6 +78,9 @@
 
     def z_dev(t):
         return {"mem": ((zi + t) % outer) * inner + xi}
+
+    def at_z(z):
+        return {"mem": z * inner + xi}
 
     barrier = pltpu.get_barrier_semaphore()
     for t in range(1, groups):
@@ -193,15 +204,25 @@
     def over_x(q, r):
         for t in range(1, inner):
             remote(x_in.at[q, r, t - 1], x_in.at[q, r, t - 1], sem_x, (q, r, t - 1), x_dev(t)).wait_recv()
-        for t in [*range(1, outer), 0]:
-            zt = (zi + t) % outer
-            span = pl.ds(pl.multiple_of(zt * part, part), part)
-            total = sums[q, r, xi, span, :].astype(jnp.float32)
-            for u in range(inner - 1):
-                total = total + x_in[q, r, u, span, :].astype(jnp.float32)
-            half[q, r, zt] = total.astype(jnp.bfloat16)
-            if t:
-                send(half.at[q, r, zt], z_in.at[q, r, t - 1], sem_z, (q, r, t - 1), z_dev(t))
+        for near in (True, False):
+            which = 1 - side if near else side
+            for duo_to in range(duos):
+                zt = 2 * duo_to + which
+                span = pl.ds(pl.multiple_of(zt * part, part), part)
+                total = sums[q, r, xi, span, :].astype(jnp.float32)
+                for u in range(inner - 1):
+                    total = total + x_in[q, r, u, span, :].astype(jnp.float32)
+                half[q, r, which, duo_to] = total.astype(jnp.bfloat16)
+            if near:
+                send(half.at[q, r, which], z_near.at[q, r], sem_z, (q, r, 0), at_z(next_z))
+
+    def near_z(q, r):
+        remote(z_near.at[q, r], z_near.at[q, r], sem_z, (q, r, 0), at_z(next_z)).wait_recv()
+        for t in range(1, duos):
+            to = (duo + t) % duos
+            total = half[q, r, side, to].astype(jnp.float32) + z_near[q, r, to].astype(jnp.float32)
+            pair[q, r, t - 1] = total.astype(jnp.bfloat16)
+            send(pair.at[q, r, t - 1], z_far.at[q, r, t - 1], sem_z, (q, r, t), at_z(far_z(t)))
 
     def codes_over_x():
         for t in range(1, inner):
@@ -228,29 +249,45 @@
         return jnp.maximum(jnp.sum(tally, axis=1, keepdims=True), 1.0)
 
     def over_z(q, r):
-        for t in range(1, outer):
-            remote(z_in.at[q, r, t - 1], z_in.at[q, r, t - 1], sem_z, (q, r, t - 1), z_dev(t)).wait_recv()
-        total = half[q, r, zi].astype(jnp.float32)
-        for u in range(outer - 1):
-            total = total + z_in[q, r, u].astype(jnp.float32)
+        for t in range(1, duos):
+            remote(
+                z_far.at[q, r, t - 1], z_far.at[q, r, t - 1], sem_z, (q, r, t), at_z(far_z(t))
+            ).wait_recv()
+        total = half[q, r, side, duo].astype(jnp.float32) + z_near[q, r, duo].astype(jnp.float32)
+        for u in range(duos - 1):
+            total = total + z_far[q, r, u].astype(jnp.float32)
         cent[q, xi, r, zi] = (total / tallies[r]).astype(jnp.bfloat16)
         block = cent.at[q, xi, r, zi]
-        for t in range(1, outer):
-            send(block, block, sem_zc, (q, r, t - 1), z_dev(t))
-        for t in range(1, inner):
-            send(block, block, sem_xc, (q, r, 0, t - 1), x_dev(t))
+        for t in range(1, duos):
+            send(block, block, sem_zc, (q, r, t), at_z(far_z(t)))
+        send(block, block, sem_zc, (q, r, 0), at_z(next_z))
+        for u in range(1, inner):
+            send(block, block, sem_xc, (q, r, 0, u - 1), x_dev(u))
+
+    def from_z(q, r, z, number, relay):
+        block = cent.at[q, xi, r, z]
+        remote(block, block, sem_zc, (q, r, number), at_z(next_z)).wait_recv()
+        if relay:
+            send(block, block, sem_zc, (q, r, duos + number - 1), at_z(next_z))
+        for u in range(1, inner):
+            send(block, block, sem_xc, (q, r, number + 1, u - 1), x_dev(u))
 
     def back_over_z(q, r):
-        for t in range(1, outer):
-            block = cent.at[q, xi, r, (zi - t + outer) % outer]
-            remote(block, block, sem_zc, (q, r, t - 1), z_dev(t)).wait_recv()
-            for u in range(1, inner):
-                send(block, block, sem_xc, (q, r, t, u - 1), x_dev(u))
+        from_z(q, r, next_z, 0, False)
+        for t in range(1, duos):
+            from_z(q, r, 2 * ((duo - t + duos) % duos) + side, t, True)
+
+    def back_near(q, r):
+        for t in range(1, duos):
+            from_z(q, r, 2 * ((duo - t + duos) % duos) + 1 - side, duos + t - 1, False)
+
+    behind = [2 * ((duo - t + duos) % duos) for t in range(1, duos)]
+    origins = [zi, next_z, *(z + side for z in behind), *(z + 1 - side for z in behind)]
 
     def back_over_x(q, r):
         for t in range(outer):
             for u in range(1, inner):
-                block = cent.at[q, (xi - u + inner) % inner, r, (zi - t + outer) % outer]
+                block = cent.at[q, (xi - u + inner) % inner, r, origins[t]]
                 remote(block, block, sem_xc, (q, r, t, u - 1), x_dev(u)).wait_recv()
         for x in range(inner):
             keep(cent.at[q, x, r], cent_out.at[q, x, r], 2 + blocks + (q * PIECES + r) * inner + x)
@@ -276,9 +313,9 @@
         for r in range(PIECES):
             sum_at = 22.0 * q + r
             x_at = 22.0 * q + 12.0 + 11.0 * r
-            stages = (add_up, over_x, over_z, back_over_z, back_over_x)
+            stages = (add_up, over_x, near_z, over_z, back_over_z, back_near, back_over_x)
             for number, stage in enumerate(stages):
-                when = sum_at if number == 0 else x_at + 12.0 * (number - 1)
+                when = sum_at if number == 0 else x_at + 9.0 * (number - 1)
                 tasks.append((when / 2.0, number, stage, (q, r)))
     tasks.append((1.5, 9, codes_over_x, ()))
     tasks.append((8.5, 9, codes_over_z, ()))
@@ -365,8 +402,10 @@
             vmem((WIDTH, slots), bf16),
             vmem((blocks, PIECES, inner, tall, cols), bf16),
             vmem((blocks, PIECES, inner - 1, tall, cols), bf16),
-            vmem((blocks, PIECES, outer, part, cols), bf16),
-            vmem((blocks, PIECES, outer - 1, part, cols), bf16),
+            vmem((blocks, PIECES, 2, outer // 2, part, cols), bf16),
+            vmem((blocks, PIECES, outer // 2, part, cols), bf16),
+            vmem((blocks, PIECES, outer // 2 - 1, part, cols), bf16),
+            vmem((blocks, PIECES, outer // 2 - 1, part, cols), bf16),
             vmem((blocks, inner, PIECES, outer, part, cols), bf16),
             vmem((WIDTH, 128), jnp.float32),
             vmem((8, WIDTH), jnp.float32),

time: 116 us -> 106 us (0.914)
  the two profiles are of different devices: /device:TPU:25 before, /device:TPU:12 now
where the time goes in v4:
time: 106 us
  Pallas kernels  106 us (100%)
    pallas_call x1, Pallas kernels, body(): pl.pallas_call(functools.partial(exchange_kernel, dims), out_shape=(jax.S...  94.3 us
    pallas_call x1, Pallas kernels, body(): pl.pallas_call(functools.partial(distance_kernel, depth), grid=(groups,),...  11.3 us

profile of v4, /device:TPU:12, one launch (start us, length us, event | category | flops | bytes accessed | tf_op | source)
XLA Modules:
  0.0 105.6 jit_solution(15844494995436807527)
XLA Ops:
  0.0 94.3 %shard_map.46 = (bf16[3,4,512,256]{3,2,1,0:T(8,128)(2,1)}, bf16[3,2,2,4,128,256]{5,4,3,2,1,0:T(8,128)(2,1)}, s32[8,512]{1,0:T(8,128)}, f32[8,2048]{1,0:T(8,128)}) custom-call(s32[1,4]{1,0:T(1,128)} %counts_ref.1, bf16[1024,768]{1,0:T(8,128)(2,1)} %vec_ref.1, s32[1,1024]{1,0:T(1,128)} %bitcast.6, s32[1,1024]{1,0:T(1,128)} %bitcast.7), custom_call_target="tpu_custom_call" | custom-call | tf_op jit(solution)/shard_map/pallas_call | solution.py:380
  94.3 11.3 %shard_map.47 = f32[2048,1024]{1,0:T(8,128)} custom-call(bf16[3,2048,256]{2,1,0:T(8,128)(2,1)} %bitcast.4, bf16[3,2048,256]{2,1,0:T(8,128)(2,1)} %bitcast.5, s32[8,512]{1,0:T(8,128)} %get-tuple-element.11.code_ref, f32[8,2048]{1,0:T(8,128)} %get-tuple-element.12.norm_ref), custom_call_target="tpu_custom_call" | custom-call | tf_op jit(solution)/shard_map/pallas_call | solution.py:428

commit v5 on v4

--- a/solution.py
+++ b/solution.py
@@ -12,7 +12,8 @@
 WIDTH = PAR_GRP * CHILD
 LOW = 32
 MIB = 1024 * 1024
-PIECES = 2
+PIECES = 4
+TOGETHER = 2
 
 
 def inner_size(members):
@@ -193,13 +194,15 @@
         for t in [*range(1, inner), 0]:
             xt = (xi + t) % inner
             total = jnp.dot(
-                member[pl.ds(pl.multiple_of(xt * share + r * tall, tall), tall), :],
+                member[pl.ds(pl.multiple_of(xt * share + r * tall, tall), TOGETHER * tall), :],
                 arrived[q].reshape(slots, cols),
                 preferred_element_type=jnp.float32,
-            )
-            sums[q, r, xt] = total.astype(jnp.bfloat16)
-            if t:
-                send(sums.at[q, r, xt], x_in.at[q, r, t - 1], sem_x, (q, r, t - 1), x_dev(t))
+            ).astype(jnp.bfloat16)
+            for place in range(TOGETHER):
+                at = r + place
+                sums[q, at, xt] = total[place * tall : (place + 1) * tall]
+                if t:
+                    send(sums.at[q, at, xt], x_in.at[q, at, t - 1], sem_x, (q, at, t - 1), x_dev(t))
 
     def over_x(q, r):
         for t in range(1, inner):
@@ -312,16 +315,17 @@
     for q in range(blocks):
         for r in range(PIECES):
             sum_at = 22.0 * q + r
-            x_at = 22.0 * q + 12.0 + 11.0 * r
+            x_at = 22.0 * q + 7.0 + 6.0 * r
             stages = (add_up, over_x, near_z, over_z, back_over_z, back_near, back_over_x)
             for number, stage in enumerate(stages):
-                when = sum_at if number == 0 else x_at + 9.0 * (number - 1)
-                tasks.append((when / 2.0, number, stage, (q, r)))
+                when = sum_at if number == 0 else x_at + 6.0 * (number - 1)
+                if number or r % TOGETHER == 0:
+                    tasks.append((when / 2.0, number, stage, (q, r)))
     tasks.append((1.5, 9, codes_over_x, ()))
-    tasks.append((8.5, 9, codes_over_z, ()))
+    tasks.append((7.5, 9, codes_over_z, ()))
     tallies = []
     for r in range(PIECES):
-        tasks.append((8.6 + r / 10, 9, lambda number: tallies.append(count_children(number)), (r,)))
+        tasks.append((7.6 + r / 10, 9, lambda number: tallies.append(count_children(number)), (r,)))
     for when, number, stage, where in sorted(tasks, key=lambda task: task[:2]):
         stage(*where)
 

time: 106 us -> 113 us (1.066)
  Pallas kernels: 106 us -> 113 us
    pallas_call x1, Pallas kernels: 94.3 us -> 101 us  [body(): pl.pallas_call(functools.partial(exchange_kernel, dims), out_shape=(jax.S...]
where the time goes in v5:
time: 113 us
  Pallas kernels  113 us (100%)
    pallas_call x1, Pallas kernels, body(): pl.pallas_call(functools.partial(exchange_kernel, dims), out_shape=(jax.S...  101 us
    pallas_call x1, Pallas kernels, body(): pl.pallas_call(functools.partial(distance_kernel, depth), grid=(groups,),...  11.3 us

profile of v5, /device:TPU:12, one launch (start us, length us, event | category | flops | bytes accessed | tf_op | source)
XLA Modules:
  0.0 112.7 jit_solution(15284162380826141894)
XLA Ops:
  0.0 101.4 %shard_map.46 = (bf16[3,4,512,256]{3,2,1,0:T(8,128)(2,1)}, bf16[3,2,4,4,64,256]{5,4,3,2,1,0:T(8,128)(2,1)}, s32[8,512]{1,0:T(8,128)}, f32[8,2048]{1,0:T(8,128)}) custom-call(s32[1,4]{1,0:T(1,128)} %counts_ref.1, bf16[1024,768]{1,0:T(8,128)(2,1)} %vec_ref.1, s32[1,1024]{1,0:T(1,128)} %bitcast.6, s32[1,1024]{1,0:T(1,128)} %bitcast.7), custom_call_target="tpu_custom_call" | custom-call | tf_op jit(solution)/shard_map/pallas_call | solution.py:384
  101.4 11.3 %shard_map.47 = f32[2048,1024]{1,0:T(8,128)} custom-call(bf16[3,2048,256]{2,1,0:T(8,128)(2,1)} %bitcast.4, bf16[3,2048,256]{2,1,0:T(8,128)(2,1)} %bitcast.5, s32[8,512]{1,0:T(8,128)} %get-tuple-element.11.code_ref, f32[8,2048]{1,0:T(8,128)} %get-tuple-element.12.norm_ref), custom_call_target="tpu_custom_call" | custom-call | tf_op jit(solution)/shard_map/pallas_call | solution.py:432
